TPU v7x, 512 devices: a whole 4x8x8 slice. The times are simulated.
512 devices in a mesh: gx: 32 (over z, x), gy: 16 (over y, core).
Axes of the slice: x: 4, y: 8, z: 8, core: 2. Of those that a mesh axis runs over, the one named last changes fastest.
Arguments:
- density: float32 [4, 128, 256, 128], P(None, 'gx', 'gy'), may hold values from 0 to 12, as said below
- rate_table: float32 [4, 9], replicated, may hold values from 0 to 128, as said below
Outputs:
- propagated: float32 [4, 128, 256, 128], P(None, 'gx', 'gy')
- step_entries: float32 [4, 5], replicated
Inputs may be any that keep to these rules, and one draw needn't show every extreme that they name: `density`: every entry is positive. `rate_table`: all entries positive; entry r of a row is the constant cr of the steps.
All inputs are finite; a program needn't handle non-finite values.
Results may differ from a plain program's by a relative error of at most 0.0006.
Values sent between devices are 32-bit elements; how exact they have to be, the bound alone decides.
A program may use at most 64 MiB of HBM per device.

v0:
```python
import jax
import jax.numpy as jnp
from jax import lax
from jax.sharding import PartitionSpec as P

tau_step = 0.01
taylor_terms = 16
squarings = 4


def padded_2(array, sides, width):
    for axis, dim in sides:
        size, length = (lax.axis_size(axis), array.shape[dim])
        up = [(i, (i + 1) % size) for i in range(size - 1)]
        down = [(j, i) for i, j in up]
        last = lax.slice_in_dim(array, length - width, length, axis=dim)
        initial = lax.slice_in_dim(array, 0, width, axis=dim)
        before = lax.ppermute(last, axis, up)
        after = lax.ppermute(initial, axis, down)
        array = jnp.concatenate([before, array, after], axis=dim)
    return array


def shift_down(vector_field):
    return jnp.concatenate([jnp.zeros_like(vector_field[..., :1]), vector_field[..., :-1]], axis=-1)


def shift_up(vector_field):
    return jnp.concatenate([vector_field[..., 1:], jnp.zeros_like(vector_field[..., :1])], axis=-1)


def generator_apply(padded, first_i, first_j, member_rates):
    row_count = padded.shape[0] - 4
    col_count = padded.shape[1] - 2
    lattice_depth = padded.shape[2]
    amount_i = (first_i + jnp.arange(row_count, dtype=jnp.int32)).astype(jnp.float32)[:, None, None]
    amount_j = (first_j + jnp.arange(col_count, dtype=jnp.int32)).astype(jnp.float32)[None, :, None]
    amount_k = jnp.arange(lattice_depth, dtype=jnp.int32).astype(jnp.float32)[None, None, :]
    ratio_j = amount_j / member_rates[7]
    ratio_k = amount_k / member_rates[8]
    make_u = member_rates[0] / (1.0 + ratio_j * ratio_j)
    make_v = member_rates[2] / (1.0 + ratio_k * ratio_k)
    outflow = make_u + member_rates[1] * amount_i + make_v + member_rates[3] * amount_j
    outflow = (
        outflow
        + 0.5 * member_rates[4] * amount_i * (amount_i - 1.0)
        + (member_rates[5] + member_rates[6]) * amount_k
    )
    centre = padded[2:-2, 1:-1]
    inflow = make_u * padded[1:-3, 1:-1]
    inflow = inflow + member_rates[1] * (amount_i + 1.0) * padded[3:-1, 1:-1]
    inflow = inflow + make_v * padded[2:-2, :-2]
    inflow = inflow + member_rates[3] * (amount_j + 1.0) * padded[2:-2, 2:]
    inflow = inflow + 0.5 * member_rates[4] * (amount_i + 2.0) * (amount_i + 1.0) * shift_down(
        padded[4:, 1:-1]
    )
    inflow = inflow + member_rates[5] * (amount_k + 1.0) * shift_up(padded[:-4, 1:-1])
    inflow = inflow + member_rates[6] * (amount_k + 1.0) * shift_up(centre)
    return inflow - outflow * centre


def matrix_exponential(small):
    scaled = small * (tau_step / 2.0**squarings)
    identity = jnp.eye(3, dtype=jnp.float32)
    series = identity + jnp.zeros_like(scaled)
    for term_index in range(taylor_terms, 0, -1):
        series = (
            identity
            + jnp.einsum("...ab,...bc->...ac", scaled, series, precision=lax.Precision.HIGHEST)
            / term_index
        )
    for square_index in range(squarings):
        series = jnp.einsum("...ab,...bc->...ac", series, series, precision=lax.Precision.HIGHEST)
    return series


def expand(values):
    return values[:, None, None, None]


def member_sum(left, right):
    return jnp.sum(left * right, axis=(1, 2, 3))


def shards(density, rate_table):
    row_count = density.shape[1]
    col_count = density.shape[2]
    first_i = lax.axis_index("gx") * row_count
    first_j = lax.axis_index("gy") * col_count
    batched = jax.vmap(generator_apply, in_axes=(0, None, None, 0))

    def shallow_image(vector_field):
        widened = padded_2(vector_field, (("gy", 2),), 1)
        padded = padded_2(widened, (("gx", 1),), 2)
        return batched(padded, first_i, first_j, rate_table)

    image_one = shallow_image(density)

    def inner_sum(left, right):
        return lax.psum(member_sum(left, right), ("gx", "gy"))

    def norm_of(vector_field):
        return jnp.sqrt(lax.psum(member_sum(vector_field, vector_field), ("gx", "gy")))

    basis_scale = jnp.sqrt(lax.psum(member_sum(density, density), ("gx", "gy")))
    basis_zero = density / expand(basis_scale)
    candidate = image_one / expand(basis_scale)
    entry_00 = inner_sum(basis_zero, candidate)
    candidate = candidate - expand(entry_00) * basis_zero
    entry_10 = norm_of(candidate)
    basis_one = candidate / expand(entry_10)
    candidate = shallow_image(basis_one)
    entry_01 = inner_sum(basis_zero, candidate)
    candidate = candidate - expand(entry_01) * basis_zero
    entry_11 = inner_sum(basis_one, candidate)
    candidate = candidate - expand(entry_11) * basis_one
    entry_21 = norm_of(candidate)
    basis_two = candidate / expand(entry_21)
    zeros = jnp.zeros_like(entry_00)
    small = jnp.stack(
        [
            jnp.stack([entry_00, entry_01, zeros], -1),
            jnp.stack([entry_10, entry_11, zeros], -1),
            jnp.stack([zeros, entry_21, zeros], -1),
        ],
        -2,
    )
    propagator = matrix_exponential(small)
    propagated = expand(basis_scale) * (
        expand(propagator[:, 0, 0]) * basis_zero
        + expand(propagator[:, 1, 0]) * basis_one
        + expand(propagator[:, 2, 0]) * basis_two
    )
    step_entries = tau_step * jnp.stack([entry_00, entry_10, entry_01, entry_11, entry_21], -1)
    return (propagated, step_entries)


def solution(mesh):
    in_specs = (P(None, "gx", "gy", None), P())
    out_specs = (P(None, "gx", "gy", None), P())
    return jax.shard_map(shards, mesh=mesh, in_specs=in_specs, out_specs=out_specs, check_vma=False)
```

profile of v0, /device:TPU:1, one launch (start us, length us, event | category | flops | bytes accessed | tf_op | source)
XLA Modules:
  0.0 624.7 jit_solution(18076800326916863573)
XLA Ops:
  0.6 0.9 fusion.70
  1.6 4.6 collective-permute-start
  6.2 5.5 collective-permute-start.1
  11.8 1.0 multiply_reduce_fusion.5
  12.8 0.3 slice_reduce_fusion.7
  13.4 1.3 collective-permute-start.2
  14.7 1.3 collective-permute-start.3
  16.1 106.7 %psum.42 = f32[4]{0:T(128)S(1)} all-reduce(f32[4]{0:T(128)S(1)} %multiply_reduce_fusion.5), channel_id=1, replica_groups=mesh['gx'=32,'gy'=16] {'gx','gy'}, use_global_device_ids=true, to_apply=%region_1.0 | all-reduce | flops 4 | bytes 32 | tf_op jit(solution)/shard_map/psum | solution.py:105
  123.0 0.4 multiply_reduce_fusion.4
  123.4 95.3 %psum.43 = f32[4]{0:T(128)S(1)} all-reduce(f32[4]{0:T(128)S(1)} %get-tuple-element.20), channel_id=1, replica_groups=mesh['gx'=32,'gy'=16] {'gx','gy'}, use_global_device_ids=true, to_apply=%region_3.0 | all-reduce | flops 4 | bytes 32 | tf_op jit(solution)/shard_map/psum | solution.py:100
  218.7 0.2 multiply_reduce_fusion.3
  218.9 93.6 %psum.44 = f32[4]{0:T(128)S(1)} all-reduce(f32[4]{0:T(128)S(1)} %multiply_reduce_fusion.3), channel_id=1, replica_groups=mesh['gx'=32,'gy'=16] {'gx','gy'}, use_global_device_ids=true, to_apply=%region_5.0 | all-reduce | flops 4 | bytes 32 | tf_op jit(solution)/shard_map/psum | solution.py:103
  312.6 3.9 collective-permute-start.4
  316.5 1.9 collective-permute-start.5
  318.4 3.0 collective-permute-done.5
  321.5 3.6 collective-permute-start.6
  325.2 1.3 collective-permute-start.7
  326.6 0.2 collective-permute-done.6
  326.8 3.7 collective-permute-done.7
  330.6 0.4 multiply_reduce_fusion.2
  330.9 98.8 %psum.45 = f32[4]{0:T(128)S(1)} all-reduce(f32[4]{0:T(128)S(1)} %get-tuple-element.18), channel_id=1, replica_groups=mesh['gx'=32,'gy'=16] {'gx','gy'}, use_global_device_ids=true, to_apply=%region_7.0 | all-reduce | flops 4 | bytes 32 | tf_op jit(solution)/shard_map/psum | solution.py:100
  429.7 0.2 multiply_reduce_fusion.1
  429.9 94.7 %psum.46 = f32[4]{0:T(128)S(1)} all-reduce(f32[4]{0:T(128)S(1)} %multiply_reduce_fusion.1), channel_id=1, replica_groups=mesh['gx'=32,'gy'=16] {'gx','gy'}, use_global_device_ids=true, to_apply=%region_9.0 | all-reduce | flops 4 | bytes 32 | tf_op jit(solution)/shard_map/psum | solution.py:100
  524.6 0.2 multiply_reduce_fusion
  524.8 94.7 %psum.47 = f32[4]{0:T(128)S(1)} all-reduce(f32[4]{0:T(128)S(1)} %multiply_reduce_fusion), channel_id=1, replica_groups=mesh['gx'=32,'gy'=16] {'gx','gy'}, use_global_device_ids=true, to_apply=%region_11.0 | all-reduce | flops 4 | bytes 32 | tf_op jit(solution)/shard_map/psum | solution.py:103
  619.5 0.7 copy.11
  620.6 0.2 fusion.13
  620.8 0.2 fusion.12
  620.9 0.2 fusion.11
  622.0 0.2 fusion.5
  622.6 0.2 fusion.1
  623.9 0.8 add_multiply_fusion
  (57 shorter events, 3.7 us)
Async XLA Ops:
  0.6 12.7 %copy-start = (f32[4,4,16,128]{3,2,1,0:T(8,128)S(1)}, f32[4,4,16,128]{3,2,1,0:T(8,128)}, u32[]{:S(2)}) copy-start(f32[4,4,16,128]{3,2,1,0:T(8,128)} %param.2) | copy-start | bytes 393220
  1.6 11.8 %collective-permute-start = (f32[4,4,1,128]{3,2,1,0:T(1,128)S(1)}, f32[4,4,1,128]{3,2,1,0:T(1,128)S(1)}, u32[]{:S(2)}, u32[]{:S(2)}) collective-permute-start(f32[4,4,1,128]{3,2,1,0:T(1,128)S(1)} %get-tuple-element.28), channel_id=1, source_target_pairs={{0,1},{1,2},{2,3},{3,4},{4,5},{5,6},{6,7},{7,8},{8,9},{9,10},{10,1... | collective-permute-start | bytes 24584 | tf_op jit(solution)/shard_map/ppermute | solution.py:18
  6.2 7.2 %collective-permute-start.1 = (f32[4,4,1,128]{3,2,1,0:T(1,128)S(1)}, f32[4,4,1,128]{3,2,1,0:T(1,128)S(1)}, u32[]{:S(2)}, u32[]{:S(2)}) collective-permute-start(f32[4,4,1,128]{3,2,1,0:T(1,128)S(1)} %get-tuple-element.29), channel_id=1, source_target_pairs={{1,0},{2,1},{3,2},{4,3},{5,4},{6,5},{7,6},{8,7},{9,8},{10,9},{11,1... | collective-permute-start | bytes 24584 | tf_op jit(solution)/shard_map/ppermute | solution.py:19
  11.7 1.0 copy-start.1
  13.4 109.5 %collective-permute-start.2 = (f32[4,2,18,128]{3,2,1,0:T(8,128)S(1)}, f32[4,2,18,128]{3,2,1,0:T(8,128)S(1)}, u32[]{:S(2)}, u32[]{:S(2)}) collective-permute-start(f32[4,2,18,128]{3,2,1,0:T(8,128)S(1)} %get-tuple-element.25), channel_id=1, source_target_pairs={{0,16},{16,32},{32,48},{48,64},{64,80},{80,96},{96,112},{112,128},... | collective-permute-start | bytes 221192 | tf_op jit(solution)/shard_map/ppermute | solution.py:18
  14.7 108.2 %collective-permute-start.3 = (f32[4,2,18,128]{3,2,1,0:T(8,128)S(1)}, f32[4,2,18,128]{3,2,1,0:T(8,128)S(1)}, u32[]{:S(2)}, u32[]{:S(2)}) collective-permute-start(f32[4,2,18,128]{3,2,1,0:T(8,128)S(1)} %get-tuple-element.24), channel_id=1, source_target_pairs={{16,0},{32,16},{48,32},{64,48},{80,64},{96,80},{112,96},{128,112},... | collective-permute-start | bytes 221192 | tf_op jit(solution)/shard_map/ppermute | solution.py:19
  312.6 5.9 collective-permute-start.4
  316.5 5.0 collective-permute-start.5
  321.5 5.3 collective-permute-start.6
  325.2 5.4 collective-permute-start.7
where the time goes:
time: 626 us; the launch traced here: 625 us
  blocking collectives  584 us (93%)
  starting transfers between devices  23.5 us (4%)
  waiting for transfers between devices  7.01 us (1%)
    psum x3, blocking collectives, inner_sum(): return lax.psum(member_sum(left, right), ('gx', 'gy'))  289 us
    psum x2, blocking collectives, norm_of(): lax.psum(member_sum(vector_field, vector_field), ('gx', 'gy'))  188 us
    psum x1, blocking collectives, shards(): basis_scale = jnp.sqrt(lax.psum(member_sum(density, density), ('gx', 'gy')))  107 us
    ppermute x4, starting transfers between devices, padded_2(): before = lax.ppermute(last, axis, up)  13.5 us
  transfers between devices with their start and end apart: 8, of which 3 were waited for; matrix products, arithmetic and copies ran while one was open for 0% of the time, Pallas kernels for 0%

commit v1 on v0

--- a/solution.py
+++ b/solution.py
@@ -2,6 +2,7 @@
 import jax.numpy as jnp
 from jax import lax
 from jax.sharding import PartitionSpec as P
+from jax.lax import psum
 
 tau_step = 0.01
 taylor_terms = 16
@@ -102,7 +103,7 @@
     def norm_of(vector_field):
         return jnp.sqrt(lax.psum(member_sum(vector_field, vector_field), ("gx", "gy")))
 
-    basis_scale = jnp.sqrt(lax.psum(member_sum(density, density), ("gx", "gy")))
+    basis_scale = jnp.sqrt(psum(psum(member_sum(density, density), "gx"), axis_name="gy"))
     basis_zero = density / expand(basis_scale)
     candidate = image_one / expand(basis_scale)
     entry_00 = inner_sum(basis_zero, candidate)

time: 626 us -> 624 us (level)
    psum x1 -> x2, blocking collectives: 107 us -> 101 us  [the longest x1 63.1 us: shards(): psum(member_sum(density, density), 'gx')]
where the time goes in v1:
time: 624 us; the launch traced here: 623 us
  blocking collectives  584 us (94%)
  starting transfers between devices  21.3 us (3%)
  waiting for transfers between devices  7.01 us (1%)
    psum x3, blocking collectives, inner_sum(): return lax.psum(member_sum(left, right), ('gx', 'gy'))  293 us
    psum x2, blocking collectives, norm_of(): lax.psum(member_sum(vector_field, vector_field), ('gx', 'gy'))  190 us
    psum x1, blocking collectives, shards(): psum(member_sum(density, density), 'gx')  63.1 us
    psum x1, blocking collectives, shards(): psum(psum(member_sum(density, density), 'gx'), axis_name='gy')  38.3 us
  transfers between devices with their start and end apart: 8, of which 3 were waited for; matrix products, arithmetic and copies ran while one was open for 0% of the time, Pallas kernels for 0%

profile of v1, /device:TPU:1, one launch (start us, length us, event | category | flops | bytes accessed | tf_op | source)
XLA Modules:
  0.0 623.2 jit_solution(16141073609000647724)
XLA Ops:
  0.6 0.9 fusion.70
  1.6 4.6 collective-permute-start
  6.2 5.5 collective-permute-start.1
  11.8 1.0 multiply_reduce_fusion.5
  12.8 0.3 slice_reduce_fusion.7
  13.3 63.1 %psum.49 = f32[4]{0:T(128)S(1)} all-reduce(f32[4]{0:T(128)S(1)} %multiply_reduce_fusion.5), channel_id=1, replica_groups=mesh['gx'=32,'gy'=16] {'gx'}, use_global_device_ids=true, to_apply=%region_1.0 | all-reduce | flops 4 | bytes 32 | tf_op jit(solution)/shard_map/psum | solution.py:106
  76.5 1.3 collective-permute-start.2
  77.8 1.3 collective-permute-start.3
  79.2 38.3 %psum.50 = f32[4]{0:T(128)S(1)} all-reduce(f32[4]{0:T(128)S(1)} %psum.49), channel_id=1, replica_groups=mesh['gx'=32,'gy'=16] {'gy'}, use_global_device_ids=true, to_apply=%region_2.0 | all-reduce | flops 4 | bytes 32 | tf_op jit(solution)/shard_map/psum | solution.py:106
  117.6 0.4 multiply_reduce_fusion.4
  118.0 97.8 %psum.51 = f32[4]{0:T(128)S(1)} all-reduce(f32[4]{0:T(128)S(1)} %get-tuple-element.20), channel_id=1, replica_groups=mesh['gx'=32,'gy'=16] {'gx','gy'}, use_global_device_ids=true, to_apply=%region_4.0 | all-reduce | flops 4 | bytes 32 | tf_op jit(solution)/shard_map/psum | solution.py:101
  215.8 0.2 multiply_reduce_fusion.3
  216.0 95.5 %psum.52 = f32[4]{0:T(128)S(1)} all-reduce(f32[4]{0:T(128)S(1)} %multiply_reduce_fusion.3), channel_id=1, replica_groups=mesh['gx'=32,'gy'=16] {'gx','gy'}, use_global_device_ids=true, to_apply=%region_6.0 | all-reduce | flops 4 | bytes 32 | tf_op jit(solution)/shard_map/psum | solution.py:104
  311.6 2.5 collective-permute-start.4
  314.1 1.9 collective-permute-start.5
  316.1 3.0 collective-permute-done.5
  319.2 2.9 collective-permute-start.6
  322.1 1.3 collective-permute-start.7
  323.5 0.2 collective-permute-done.6
  323.7 3.7 collective-permute-done.7
  327.5 0.4 multiply_reduce_fusion.2
  327.8 100.3 %psum.53 = f32[4]{0:T(128)S(1)} all-reduce(f32[4]{0:T(128)S(1)} %get-tuple-element.18), channel_id=1, replica_groups=mesh['gx'=32,'gy'=16] {'gx','gy'}, use_global_device_ids=true, to_apply=%region_8.0 | all-reduce | flops 4 | bytes 32 | tf_op jit(solution)/shard_map/psum | solution.py:101
  428.2 0.2 multiply_reduce_fusion.1
  428.4 94.8 %psum.54 = f32[4]{0:T(128)S(1)} all-reduce(f32[4]{0:T(128)S(1)} %multiply_reduce_fusion.1), channel_id=1, replica_groups=mesh['gx'=32,'gy'=16] {'gx','gy'}, use_global_device_ids=true, to_apply=%region_10.0 | all-reduce | flops 4 | bytes 32 | tf_op jit(solution)/shard_map/psum | solution.py:101
  523.2 0.2 multiply_reduce_fusion
  523.4 94.6 %psum.55 = f32[4]{0:T(128)S(1)} all-reduce(f32[4]{0:T(128)S(1)} %multiply_reduce_fusion), channel_id=1, replica_groups=mesh['gx'=32,'gy'=16] {'gx','gy'}, use_global_device_ids=true, to_apply=%region_12.0 | all-reduce | flops 4 | bytes 32 | tf_op jit(solution)/shard_map/psum | solution.py:104
  618.0 0.7 copy.11
  619.1 0.2 fusion.13
  619.3 0.2 fusion.12
  620.5 0.2 fusion.5
  621.1 0.2 fusion.1
  622.4 0.8 add_multiply_fusion
  (58 shorter events, 3.9 us)
Async XLA Ops:
  0.6 75.8 %copy-start = (f32[4,4,16,128]{3,2,1,0:T(8,128)S(1)}, f32[4,4,16,128]{3,2,1,0:T(8,128)}, u32[]{:S(2)}) copy-start(f32[4,4,16,128]{3,2,1,0:T(8,128)} %param.2) | copy-start | bytes 393220
  1.6 74.9 %collective-permute-start = (f32[4,4,1,128]{3,2,1,0:T(1,128)S(1)}, f32[4,4,1,128]{3,2,1,0:T(1,128)S(1)}, u32[]{:S(2)}, u32[]{:S(2)}) collective-permute-start(f32[4,4,1,128]{3,2,1,0:T(1,128)S(1)} %get-tuple-element.28), channel_id=1, source_target_pairs={{0,1},{1,2},{2,3},{3,4},{4,5},{5,6},{6,7},{7,8},{8,9},{9,10},{10,1... | collective-permute-start | bytes 24584 | tf_op jit(solution)/shard_map/ppermute | solution.py:19
  6.2 70.3 %collective-permute-start.1 = (f32[4,4,1,128]{3,2,1,0:T(1,128)S(1)}, f32[4,4,1,128]{3,2,1,0:T(1,128)S(1)}, u32[]{:S(2)}, u32[]{:S(2)}) collective-permute-start(f32[4,4,1,128]{3,2,1,0:T(1,128)S(1)} %get-tuple-element.29), channel_id=1, source_target_pairs={{1,0},{2,1},{3,2},{4,3},{5,4},{6,5},{7,6},{8,7},{9,8},{10,9},{11,1... | collective-permute-start | bytes 24584 | tf_op jit(solution)/shard_map/ppermute | solution.py:20
  11.7 1.0 copy-start.1
  76.5 41.1 %collective-permute-start.2 = (f32[4,2,18,128]{3,2,1,0:T(8,128)S(1)}, f32[4,2,18,128]{3,2,1,0:T(8,128)S(1)}, u32[]{:S(2)}, u32[]{:S(2)}) collective-permute-start(f32[4,2,18,128]{3,2,1,0:T(8,128)S(1)} %get-tuple-element.25), channel_id=1, source_target_pairs={{0,16},{16,32},{32,48},{48,64},{64,80},{80,96},{96,112},{112,128},... | collective-permute-start | bytes 221192 | tf_op jit(solution)/shard_map/ppermute | solution.py:19
  77.8 39.8 %collective-permute-start.3 = (f32[4,2,18,128]{3,2,1,0:T(8,128)S(1)}, f32[4,2,18,128]{3,2,1,0:T(8,128)S(1)}, u32[]{:S(2)}, u32[]{:S(2)}) collective-permute-start(f32[4,2,18,128]{3,2,1,0:T(8,128)S(1)} %get-tuple-element.24), channel_id=1, source_target_pairs={{16,0},{32,16},{48,32},{64,48},{80,64},{96,80},{112,96},{128,112},... | collective-permute-start | bytes 221192 | tf_op jit(solution)/shard_map/ppermute | solution.py:20
  311.6 4.5 collective-permute-start.4
  314.1 5.0 collective-permute-start.5
  319.2 4.6 collective-permute-start.6
  322.1 5.4 collective-permute-start.7
